TPU v7x, 32 devices: a whole 2x2x4 slice. The times are simulated.
32 devices in a mesh: wave: 8 (over y, x, core), pole: 4 (over z).
Axes of the slice: x: 2, y: 2, z: 4, core: 2. Of those that a mesh axis runs over, the one named last changes fastest.
Arguments:
- grid: float32 [6, 128, 3072], P(None, None, 'wave'), may hold values from -6 to 6
- legendre: bfloat16 [128, 2, 1536, 1024], P('wave', None, None, 'pole'), may hold values from -0.15625 to 0.15625
- wave_table: int32 [128], replicated, may hold values from 0 to 127, each once
- pole_table: float32 [4, 32], replicated, may hold values from -1.5 to 2.5, as said below
- pole_index: int32 [16], replicated, may hold values from 0 to 31
Outputs:
- next_state: float32 [6, 2, 128, 1024], P(None, None, 'wave', 'pole')
Inputs may be any that keep to these rules, and one draw needn't show every extreme that they name: Slot s holds zonal wavenumber wave_table[s], every wavenumber of 0 to 127 once; row s of legendre belongs to it. `pole_table`: shift real parts lie in 1.5 to 2.5, shift imaginary parts in -1.5 to 1.5, weights in -1.2 to 1.2.
All inputs are finite; a program needn't handle non-finite values.
Results may differ from a plain program's by a relative error of at most 0.0003.
Values sent between devices are 32-bit elements; how exact they have to be, the bound alone decides.
A program may use at most 128 MiB of HBM per device.

v0:
```python
import jax
import jax.numpy as jnp
from jax import lax
from jax.sharding import PartitionSpec as P

SWEEPS = 8


coriolis_step = 1.2
gravity_step = 0.0008


def split_high(values):
    upper_part = values.astype(jnp.bfloat16)
    kept = lax.optimization_barrier(upper_part)
    lower_part = (values - kept.astype(jnp.float32)).astype(jnp.bfloat16)
    return (upper_part, lower_part)


def coefficients(wavenum, count):
    index = jnp.arange(count, dtype=jnp.int32).astype(jnp.float32)
    parity = jnp.arange(2, dtype=jnp.int32).astype(jnp.float32)
    order = (2.0 * index[None, :] + parity[:, None])[:, None, :]
    wave = wavenum[None, :, None]
    degree = wave + order
    product = degree * (degree + 1.0)
    rossby = coriolis_step * wave / jnp.maximum(product, 2.0)
    gravity = gravity_step * jnp.sqrt(product)
    e_lo = jnp.sqrt(order * (2.0 * wave + order) / jnp.maximum(4.0 * degree * degree - 1.0, 1.0))
    after = order + 1.0
    upper_deg = degree + 1.0
    e_hi = jnp.sqrt(
        after * (2.0 * wave + after) / jnp.maximum(4.0 * upper_deg * upper_deg - 1.0, 1.0)
    )
    return (e_lo, e_hi, rossby, gravity)


def cmul(are, aim, bre, bim):
    return (are * bre - aim * bim, are * bim + aim * bre)


def zero_extend(field):
    return jnp.pad(field, ((0, 0), (0, 0), (0, 0), (0, 0), (1, 1)))


def solve(spectra, coef, shifts, extend):
    e_lo, e_hi, rossby, gravity = coef
    count = spectra.shape[3]
    shift_re = shifts[:, 0][:, None, None, None]
    shift_im = shifts[:, 1][:, None, None, None]
    weight_re = shifts[:, 2][:, None, None, None]
    weight_im = shifts[:, 3][:, None, None, None]
    z0r, z0i = (spectra[0][None], spectra[1][None])
    d0r, d0i = (spectra[2][None], spectra[3][None])
    h0r, h0i = (spectra[4][None], spectra[5][None])
    b_re = shift_re + 0.0 * rossby[None]
    b_im = shift_im + rossby[None]
    b_mag = b_re * b_re + b_im * b_im
    inv_re, inv_im = (b_re / b_mag, -b_im / b_mag)
    det_re, det_im = cmul(b_re, b_im, shift_re, shift_im)
    det_re = det_re + gravity[None] * gravity[None]
    det_mag = det_re * det_re + det_im * det_im
    dinv_re, dinv_im = (det_re / det_mag, -det_im / det_mag)
    grav = gravity[None]
    hb_re, hb_im = cmul(b_re, b_im, h0r, h0i)
    zr, zi, dr, di, hr, hi = (z0r, z0i, d0r, d0i, h0r, h0i)
    for sweep in range(SWEEPS):
        if sweep == 0:
            rzr, rzi, rdr, rdi = (z0r, z0i, d0r, d0i)
        else:
            both = jnp.stack([zr, zi, dr, di], axis=0)
            ext = extend(both)
            lower = jnp.stack([ext[:, :, 1, :, 0:count], ext[:, :, 0, :, 1 : count + 1]], axis=2)
            upper = jnp.stack(
                [ext[:, :, 1, :, 1 : count + 1], ext[:, :, 0, :, 2 : count + 2]], axis=2
            )
            near = e_lo * lower + e_hi * upper
            rzr = z0r - coriolis_step * near[2]
            rzi = z0i - coriolis_step * near[3]
            rdr = d0r + coriolis_step * near[0]
            rdi = d0i + coriolis_step * near[1]
        zr, zi = cmul(rzr, rzi, inv_re, inv_im)
        nd_re, nd_im = cmul(shift_re, shift_im, rdr, rdi)
        nd_re = nd_re + grav * h0r
        nd_im = nd_im + grav * h0i
        nh_re = hb_re - grav * rdr
        nh_im = hb_im - grav * rdi
        dr, di = cmul(nd_re, nd_im, dinv_re, dinv_im)
        hr, hi = cmul(nh_re, nh_im, dinv_re, dinv_im)
    parts = []
    for field_re, field_im in ((zr, zi), (dr, di), (hr, hi)):
        out_re, out_im = cmul(weight_re, weight_im, field_re, field_im)
        parts.append(jnp.sum(out_re, axis=0))
        parts.append(jnp.sum(out_im, axis=0))
    return jnp.stack(parts, axis=0)


def lookup(pole_table, chosen):
    columns = jnp.arange(pole_table.shape[1], dtype=jnp.int32)
    onehot = (chosen[:, None] == columns[None, :]).astype(jnp.float32)
    return jnp.dot(onehot, jnp.transpose(pole_table), precision=lax.Precision.HIGHEST)


def shards(grid, legendre, wave_table, pole_table, pole_index):
    slots = legendre.shape[0]
    local_k = legendre.shape[3]
    lat_rows = grid.shape[2]
    wave_count = lax.axis_size("wave")
    half_count = wave_count // 2
    columns = jnp.take(grid, wave_table, axis=1)
    regrouped = lax.all_to_all(columns[None], "wave", split_axis=2, concat_axis=0, tiled=True)
    north = regrouped[:half_count]
    south = regrouped[half_count:]
    parts = jnp.stack([north + south, north - south], axis=0)
    high, low = split_high(parts)
    leg_blocks = legendre.reshape(slots, 2, half_count, lat_rows, local_k)
    first = jnp.einsum("mpwlk,pwcml->cpmk", leg_blocks, high, preferred_element_type=jnp.float32)
    second = jnp.einsum("mpwlk,pwcml->cpmk", leg_blocks, low, preferred_element_type=jnp.float32)
    spectra = first + second
    own_waves = lax.dynamic_slice_in_dim(wave_table, lax.axis_index("wave") * slots, slots).astype(
        jnp.float32
    )
    whole = lax.all_gather(spectra, "pole", axis=3, tiled=True)
    per_device = pole_index.shape[0] // lax.axis_size("pole")
    chosen = lax.dynamic_slice_in_dim(pole_index, lax.axis_index("pole") * per_device, per_device)
    coef = coefficients(own_waves, whole.shape[3])
    partial_terms = solve(whole, coef, lookup(pole_table, chosen), zero_extend)
    result = lax.psum_scatter(partial_terms, "pole", scatter_dimension=3, tiled=True)
    return result


def solution(mesh):
    in_specs = (P(None, None, "wave"), P("wave", None, None, "pole"), P(), P(), P())
    out_specs = P(None, None, "wave", "pole")
    return jax.shard_map(shards, mesh=mesh, in_specs=in_specs, out_specs=out_specs, check_vma=False)
```

profile of v0, /device:TPU:0, one launch (start us, length us, event | category | flops | bytes accessed | tf_op | source)
XLA Modules:
  0.0 129.5 jit_solution(8620515160245397620)
XLA Ops:
  8.0 2.4 %gather_fusion = f32[128,6,384]{2,0,1:T(8,128)S(1)} fusion(f32[6,128,384]{2,1,0:T(8,128)S(1)} %copy-done, s32[1024]{0:T(1024)S(1)} %pad_clamp_fusion), kind=kCustom, calls=%fused_computation | custom fusion | bytes 2359808 | tf_op jit(solution)/shard_map/jit(_take)/gather | solution.py:110
  10.5 2.3 %copy.21 = f32[1,6,128,384]{3,0,1,2:T(1,128)} copy(f32[1,6,128,384]{3,2,1,0:T(8,128)S(1)} %bitcast_select_fusion) | data formatting | bytes 2359296 | tf_op jit(solution)/shard_map/jit(_take)/select_n | solution.py:110
  12.8 5.2 %all-to-all-start = ((f32[1,6,128,384]{3,0,1,2:T(1,128)}), f32[1,6,128,384]{3,0,1,2:T(1,128)S(1)}, u32[]{:S(2)}, u32[]{:S(2)}) async-start(f32[1,6,128,384]{3,0,1,2:T(1,128)} %copy.21), calls=%async_computation | async-start | bytes 2359296 | tf_op jit(solution)/shard_map/all_to_all | solution.py:111
  18.8 16.0 %all-to-all-done = f32[1,6,128,384]{3,0,1,2:T(1,128)S(1)} async-done(((f32[1,6,128,384]{3,0,1,2:T(1,128)}), f32[1,6,128,384]{3,0,1,2:T(1,128)S(1)}, u32[]{:S(2)}, u32[]{:S(2)}) %all-to-all-start) | async-done | bytes 1179680 | tf_op jit(solution)/shard_map/all_to_all | solution.py:111
  35.9 10.0 %fusion.12 = f32[2,16,6,256]{3,2,1,0:T(8,128)S(1)} fusion(bf16[2,4,6,16,384]{4,2,1,3,0:T(8,128)(2,1)S(1)} %fusion.11, bf16[16,2,4,384,256]{4,3,2,1,0:T(8,128)(2,1)} %bitcast.123), kind=kOutput, calls=%fused_computation.72 | convolution fusion | flops 150994944 | bytes 25952256 | tf_op jit(solution)/shard_map/mpwlk,pwcml->cpmk/dot_general | solution.py:117
  45.9 10.0 %fusion.21 = f32[6,2,16,256]{3,0,2,1:T(8,128)S(1)} fusion(f32[2,16,6,256]{3,2,1,0:T(8,128)S(1)} %fusion.12, bf16[16,2,4,384,256]{4,3,2,1,0:T(8,128)(2,1)} %bitcast.124, bf16[2,4,6,16,384]{4,2,1,3,0:T(8,128)(2,1)S(1)} %fusion.11, f32[1,4,6,16,384]{4,2,1,3,0:T(8,128)S(1)} %get-tuple-element.86, f32[1,4,6,16,384]{4,2,1,3,0:T(8,128)S(1)} %get-tuple-element.85), kind=kOutput, calls=%fused_computation.75 | convolution fusion | flops 152223744 | bytes 27328512 | tf_op jit(solution)/shard_map/mpwlk,pwcml->cpmk/dot_general | solution.py:118
  55.8 21.8 %all_gather.3 = f32[6,2,16,1024]{3,0,2,1:T(8,128)S(1)} all-gather(f32[6,2,16,256]{3,0,2,1:T(8,128)S(1)} %fusion.21), channel_id=1, replica_groups=mesh['wave'=8,'pole'=4] {'pole'}, dimensions={3}, use_global_device_ids=true | all-gather | bytes 983040 | tf_op jit(solution)/shard_map/all_gather | solution.py:123
  77.7 0.9 fusion.99
  79.8 0.8 fusion.110
  81.2 0.9 multiply_subtract_fusion.14
  82.3 0.8 fusion.109
  83.7 0.9 multiply_subtract_fusion.12
  84.8 0.8 fusion.108
  86.1 0.9 multiply_subtract_fusion.10
  87.3 0.8 fusion.107
  88.6 0.9 multiply_subtract_fusion.8
  89.8 0.8 fusion.106
  91.3 0.9 multiply_subtract_fusion.6
  92.5 0.8 fusion.105
  93.8 0.9 multiply_subtract_fusion.4
  94.9 0.8 fusion.104
  97.4 1.1 add_reduce_fusion
  98.6 0.9 copy-done.2
  99.5 23.1 %reduce-scatter.2.cloned.1.call-done = f32[6,2,16,256]{3,2,1,0:T(8,128)} async-done(((f32[6,2,16,1024]{3,2,1,0:T(8,128)}), f32[6,2,16,256]{3,2,1,0:T(8,128)}) %reduce-scatter.2.cloned.1.call-update) | async-done | bytes 196624 | tf_op jit(solution)/shard_map/reduce_scatter | solution.py:128
  (57 shorter events, 10.9 us)
Async XLA Ops:
  6.5 1.4 %copy-start = (f32[6,128,384]{2,1,0:T(8,128)S(1)}, f32[6,128,384]{2,1,0:T(8,128)}, u32[]{:S(2)}) copy-start(f32[6,128,384]{2,1,0:T(8,128)} %param.5) | copy-start | bytes 3538948
  10.5 7.5 %copy-start.3 = (s32[128]{0:T(128)S(1)}, s32[128]{0:T(128)}, u32[]{:S(2)}) copy-start(s32[128]{0:T(128)} %param.7) | copy-start | bytes 1540
  10.5 7.6 %copy-start.5 = (s32[16]{0:T(128)S(1)}, s32[16]{0:T(128)}, u32[]{:S(2)}) copy-start(s32[16]{0:T(128)} %param.9) | copy-start | bytes 196
  10.5 7.7 %copy-start.4 = (f32[4,32]{1,0:T(4,128)S(1)}, f32[4,32]{1,0:T(4,128)}, u32[]{:S(2)}) copy-start(f32[4,32]{1,0:T(4,128)} %param.8) | copy-start | bytes 1540
  12.8 22.0 %all-to-all-start = ((f32[1,6,128,384]{3,0,1,2:T(1,128)}), f32[1,6,128,384]{3,0,1,2:T(1,128)S(1)}, u32[]{:S(2)}, u32[]{:S(2)}) async-start(f32[1,6,128,384]{3,0,1,2:T(1,128)} %copy.21), calls=%async_computation | async-start | bytes 2359296 | tf_op jit(solution)/shard_map/all_to_all | solution.py:111
  18.0 104.6 %reduce-scatter.2.cloned.1.call-start = ((), (), s32[]{:S(2)}) async-start(), calls=%async_computation.2 | async-start | bytes 983040 | tf_op jit(solution)/shard_map/reduce_scatter | solution.py:128
  97.4 25.2 %copy-start.1 = (f32[6,128,384]{2,1,0:T(8,128)S(1)}, f32[6,128,384]{2,1,0:T(8,128)}, u32[]{:S(2)}) copy-start(f32[6,128,384]{2,1,0:T(8,128)} %param.5) | copy-start | bytes 3538948
  98.6 0.9 copy-start.2
Sparse Core Ops, SparseCore 0:
  99.7 22.9 reduce-scatter.1
where the time goes:
time: 130 us; the launch traced here: 129 us
  waiting for transfers between devices  39.1 us (30%)
  blocking collectives  21.8 us (17%)
  matrix products  20.1 us (15%)
  other arithmetic  17 us (13%)
  between operations  13.7 us (11%)
  local copies, waits for them, and re-layouts  12.4 us (10%)
  starting transfers between devices  5.21 us (4%)
    reduce_scatter x1, waiting for transfers between devices, shards(): lax.psum_scatter(partial_terms, 'pole', scatter_dimension=3, tiled=True)  23.1 us
    all_gather x1, blocking collectives, shards(): whole = lax.all_gather(spectra, 'pole', axis=3, tiled=True)  21.8 us
    all_to_all x1, waiting for transfers between devices, shards(): lax.all_to_all(columns[None], 'wave', split_axis=2, concat_axis=0, tiled=...  16 us
    dot_general x1, matrix products, shards(): jnp.einsum('mpwlk,pwcml->cpmk', leg_blocks, high, preferred_element_type=...  9.96 us
    dot_general x1, matrix products, shards(): jnp.einsum('mpwlk,pwcml->cpmk', leg_blocks, low, preferred_element_type=j...  9.96 us
    sub x8, other arithmetic, cmul(): return (are * bre - aim * bim, are * bim + aim * bre)  6.75 us
    slice x7, local copies, waits for them, and re-layouts, solve(): ext[:, :, 1, :, 1:count + 1]  5.74 us
    all_to_all x1, starting transfers between devices, shards(): lax.all_to_all(columns[None], 'wave', split_axis=2, concat_axis=0, tiled=...  5.17 us
  transfers between devices with their start and end apart: 2, of which 2 were waited for; matrix products, arithmetic and copies ran while one was open for 1% of the time, Pallas kernels for 0%

commit v1 on v0

v1 whole, which is shorter than its diff:
```python
import functools

import jax
import jax.numpy as jnp
from jax import lax
from jax.experimental import pallas as pl
from jax.experimental.pallas import tpu as pltpu
from jax.sharding import PartitionSpec as P

SWEEPS = 8
GROUP = 8
HALO = 4
LANES = 128
MESH = pl.DeviceIdType.MESH

coriolis_step = 1.2
gravity_step = 0.0008


def cmul(are, aim, bre, bim):
    return (are * bre - aim * bim, are * bim + aim * bre)


def coefficients(wave, position, valid, parity):
    order = 2.0 * position + parity
    degree = wave + order
    product = degree * (degree + 1.0)
    rossby = coriolis_step * wave / jnp.maximum(product, 2.0)
    gravity = gravity_step * jnp.sqrt(product)
    e_lo = jnp.sqrt(order * (2.0 * wave + order) / jnp.maximum(4.0 * degree * degree - 1.0, 1.0))
    after = order + 1.0
    upper_deg = degree + 1.0
    e_hi = jnp.sqrt(
        after * (2.0 * wave + after) / jnp.maximum(4.0 * upper_deg * upper_deg - 1.0, 1.0)
    )
    e_lo = jnp.where(valid, coriolis_step * e_lo, 0.0)
    e_hi = jnp.where(valid, coriolis_step * e_hi, 0.0)
    return e_lo, e_hi, rossby, gravity


def kernel(
    waves,
    poles,
    grid_hbm,
    leg_hbm,
    wave_table,
    pole_table,
    pole_index,
    out_ref,
    grid_v,
    leg_v,
    send,
    recv,
    parts,
    spec,
    coef,
    halo_send,
    halo_recv,
    grid_sem,
    leg_sem,
    send_sem,
    recv_sem,
    halo_send_sem,
    halo_recv_sem,
):
    comps = grid_hbm.shape[0]
    lat = grid_hbm.shape[2]
    slots = leg_hbm.shape[0]
    count = leg_hbm.shape[3]
    groups = slots // GROUP
    half = waves // 2
    rows = GROUP * comps
    width = count + LANES
    solves = pole_index.shape[0]
    me = lax.axis_index("wave")
    zone = lax.axis_index("pole")

    barrier = pltpu.get_barrier_semaphore()
    for step in range(1, waves):
        pl.semaphore_signal(
            barrier, inc=1, device_id=(lax.rem(me + step, waves), zone), device_id_type=MESH
        )

    @pl.when(zone > 0)
    def _():
        pl.semaphore_signal(barrier, inc=1, device_id=(me, zone - 1), device_id_type=MESH)

    @pl.when(zone < poles - 1)
    def _():
        pl.semaphore_signal(barrier, inc=1, device_id=(me, zone + 1), device_id_type=MESH)

    grid_copy = pltpu.make_async_copy(grid_hbm, grid_v, grid_sem)
    grid_copy.start()
    leg_copies = [
        pltpu.make_async_copy(leg_hbm.at[s], leg_v.at[s], leg_sem.at[s]) for s in range(slots)
    ]
    for copy in leg_copies:
        copy.start()
    parts[:, :, rows:, :] = jnp.zeros((half, 2, parts.shape[2] - rows, lat), jnp.float32)
    grid_copy.wait()

    def collect(target, g, d):
        for s in range(GROUP):
            m = wave_table[d * slots + g * GROUP + s]
            for c in range(comps):
                target[g, d, s * comps + c : s * comps + c + 1, :] = grid_v[c, pl.ds(m, 1), :]

    def exchange(g, there, here):
        return pltpu.make_async_remote_copy(
            src_ref=send.at[g, there],
            dst_ref=recv.at[g, here],
            send_sem=send_sem.at[g, there],
            recv_sem=recv_sem.at[g, here],
            device_id=(there, zone),
            device_id_type=MESH,
        )

    neighbours = (zone > 0).astype(jnp.int32) + (zone < poles - 1).astype(jnp.int32)
    pl.semaphore_wait(barrier, waves - 1 + neighbours)

    for g in range(groups):

        def send_one(step, carry, g=g):
            there = lax.rem(me + step, waves)
            collect(send, g, there)
            exchange(g, there, me).start()
            return carry

        lax.fori_loop(1, waves, send_one, 0)
    for g in range(groups):
        collect(recv, g, me)

    lane = lax.broadcasted_iota(jnp.int32, (GROUP, LANES), 1)
    line = lax.broadcasted_iota(jnp.int32, (GROUP, width), 0)
    place = lax.broadcasted_iota(jnp.int32, (GROUP, width), 1)
    local = jnp.where(place >= width - HALO, place - width, place)
    k_index = local + zone * count
    valid = (local < count + HALO) & (k_index >= 0) & (k_index < poles * count)
    position = k_index.astype(jnp.float32)

    def left_copy(g):
        return pltpu.make_async_remote_copy(
            src_ref=halo_send.at[g, 0],
            dst_ref=halo_recv.at[g, 1],
            send_sem=halo_send_sem.at[g, 0],
            recv_sem=halo_recv_sem.at[g, 1],
            device_id=(me, lax.rem(zone + poles - 1, poles)),
            device_id_type=MESH,
        )

    def right_copy(g):
        return pltpu.make_async_remote_copy(
            src_ref=halo_send.at[g, 1],
            dst_ref=halo_recv.at[g, 0],
            send_sem=halo_send_sem.at[g, 1],
            recv_sem=halo_recv_sem.at[g, 0],
            device_id=(me, lax.rem(zone + 1, poles)),
            device_id_type=MESH,
        )

    def group_step(g, carry):
        wave = jnp.zeros((GROUP, width), jnp.float32)
        for s in range(GROUP):
            m = wave_table[me * slots + g * GROUP + s].astype(jnp.float32)
            wave = jnp.where(line == s, m, wave)
        for p in range(2):
            for i, value in enumerate(coefficients(wave, position, valid, float(p))):
                coef[i, p] = value

        for w in range(half):
            for source in (w, w + half):

                @pl.when(me != source)
                def _():
                    exchange(g, source, source).wait_recv()

            north = recv[g, w]
            south = recv[g, w + half]
            parts[w, 0, 0:rows, :] = north + south
            parts[w, 1, 0:rows, :] = north - south

        span = half if lat % LANES == 0 else 1
        for s in range(GROUP):
            slot = g * GROUP + s
            pltpu.make_async_copy(leg_hbm.at[slot], leg_v.at[slot], leg_sem.at[slot]).wait()

            def analyse(p, carry, s=s, slot=slot):
                total = jnp.zeros((16, count), jnp.float32)
                for first in range(0, half, span):
                    pieces = []
                    for w in range(first, first + span):
                        value = parts[w, p, s * comps : s * comps + 8, :]
                        high = value.astype(jnp.bfloat16).astype(jnp.float32)
                        pieces.append(jnp.concatenate([high, value - high], axis=0))
                    left = jnp.concatenate(pieces, axis=1) if span > 1 else pieces[0]
                    total = total + jnp.dot(
                        left.astype(jnp.bfloat16),
                        leg_v[slot, p, first * lat : (first + span) * lat, :],
                        preferred_element_type=jnp.float32,
                    )
                both = total[0:8] + total[8:16]
                for c in range(comps):
                    spec[c, p, s : s + 1, 0:count] = both[c : c + 1]
                return carry

            lax.fori_loop(0, 2, analyse, 0)

        lower = jnp.zeros((GROUP, LANES), jnp.float32)
        upper = jnp.zeros((GROUP, LANES), jnp.float32)
        for i in range(2 * comps):
            c, p = i // 2, i % 2
            mine = (lane >= HALO * i) & (lane < HALO * (i + 1))
            first = spec[c, p, :, 0:LANES]
            last = spec[c, p, :, count - LANES : count]
            lower = jnp.where(mine, pltpu.roll(first, HALO * i, 1) if i else first, lower)
            upper = jnp.where(mine, pltpu.roll(last, HALO * (i + 1), 1), upper)
        halo_send[g, 0] = lower
        halo_send[g, 1] = upper

        @pl.when(zone > 0)
        def _():
            left_copy(g).start()

        @pl.when(zone < poles - 1)
        def _():
            right_copy(g).start()

        @pl.when(zone > 0)
        def _():
            right_copy(g).wait_recv()
            left_copy(g).wait_send()

        @pl.when(zone < poles - 1)
        def _():
            left_copy(g).wait_recv()
            right_copy(g).wait_send()

        from_left = halo_recv[g, 0]
        from_right = halo_recv[g, 1]
        for i in range(2 * comps):
            c, p = i // 2, i % 2
            right = pltpu.roll(from_right, LANES - HALO * i, 1) if i else from_right
            left = pltpu.roll(from_left, LANES - HALO * (i + 1), 1)
            edge = jnp.where((lane < HALO) & (zone < poles - 1), right, 0.0)
            edge = jnp.where((lane >= LANES - HALO) & (zone > 0), left, edge)
            spec[c, p, :, count:width] = edge

        home = pl.ds(pl.multiple_of(g * GROUP, GROUP), GROUP)
        out_ref[:, :, home, :] = jnp.zeros((comps, 2, GROUP, count), jnp.float32)

        def near(field):
            even, odd = field
            first = coef[0, 0] * pltpu.roll(odd, 1, 1) + coef[1, 0] * odd
            second = coef[0, 1] * even + coef[1, 1] * pltpu.roll(even, width - 1, 1)
            return first, second

        def pole_step(q, carry):
            column = pole_index[q]
            a_re, a_im = pole_table[0, column], pole_table[1, column]
            w_re, w_im = pole_table[2, column], pole_table[3, column]
            inv, turn, z_first, d_first, dinv, b_all = [], [], [], [], [], []
            for p in range(2):
                rossby, grav = coef[2, p], coef[3, p]
                b_re = a_re + 0.0 * rossby
                b_im = a_im + rossby
                b_mag = 1.0 / (b_re * b_re + b_im * b_im)
                i_re, i_im = b_re * b_mag, -b_im * b_mag
                det_re, det_im = cmul(b_re, b_im, a_re, a_im)
                det_re = det_re + grav * grav
                det_mag = 1.0 / (det_re * det_re + det_im * det_im)
                v_re, v_im = det_re * det_mag, -det_im * det_mag
                t_re, t_im = cmul(a_re, a_im, v_re, v_im)
                g_re, g_im = cmul(v_re, v_im, grav * spec[4, p], grav * spec[5, p])
                d_re, d_im = cmul(t_re, t_im, spec[2, p], spec[3, p])
                inv.append((i_re, i_im))
                turn.append((t_re, t_im))
                dinv.append((v_re, v_im))
                b_all.append((b_re, b_im))
                z_first.append(cmul(i_re, i_im, spec[0, p], spec[1, p]))
                d_first.append((d_re + g_re, d_im + g_im))
            z, d = z_first, d_first
            for sweep in range(1, SWEEPS):
                zn_re = near((z[0][0], z[1][0]))
                zn_im = near((z[0][1], z[1][1]))
                dn_re = near((d[0][0], d[1][0]))
                dn_im = near((d[0][1], d[1][1]))
                z_next, d_next = [], []
                for p in range(2):
                    re, im = cmul(inv[p][0], inv[p][1], dn_re[p], dn_im[p])
                    z_next.append((z_first[p][0] - re, z_first[p][1] - im))
                    re, im = cmul(turn[p][0], turn[p][1], zn_re[p], zn_im[p])
                    d_next.append((d_first[p][0] + re, d_first[p][1] + im))
                z, d = z_next, d_next
            for p in range(2):
                grav = coef[3, p][:, 0:count]
                hb_re, hb_im = cmul(
                    b_all[p][0][:, 0:count],
                    b_all[p][1][:, 0:count],
                    spec[4, p, :, 0:count],
                    spec[5, p, :, 0:count],
                )
                nh_re = hb_re - grav * (spec[2, p, :, 0:count] + zn_re[p][:, 0:count])
                nh_im = hb_im - grav * (spec[3, p, :, 0:count] + zn_im[p][:, 0:count])
                h = cmul(nh_re, nh_im, dinv[p][0][:, 0:count], dinv[p][1][:, 0:count])
                for f, (re, im) in enumerate((z[p], d[p], h)):
                    o_re, o_im = cmul(w_re, w_im, re[:, 0:count], im[:, 0:count])
                    out_ref[2 * f, p, home, :] += o_re
                    out_ref[2 * f + 1, p, home, :] += o_im
            return carry

        lax.fori_loop(0, solves, pole_step, 0)
        return carry

    lax.fori_loop(0, groups, group_step, 0)

    for g in range(groups):

        def finish(step, carry, g=g):
            exchange(g, lax.rem(me + step, waves), me).wait_send()
            return carry

        lax.fori_loop(1, waves, finish, 0)


def shards(grid, legendre, wave_table, pole_table, pole_index):
    waves = lax.axis_size("wave")
    poles = lax.axis_size("pole")
    comps, _, lat = grid.shape
    slots, _, north, count = legendre.shape
    groups = slots // GROUP
    rows = GROUP * comps
    width = count + LANES
    f32 = jnp.float32
    return pl.pallas_call(
        functools.partial(kernel, waves, poles),
        out_shape=jax.ShapeDtypeStruct((comps, 2, slots, count), f32),
        in_specs=[
            pl.BlockSpec(memory_space=pl.ANY),
            pl.BlockSpec(memory_space=pl.ANY),
            pl.BlockSpec(memory_space=pltpu.SMEM),
            pl.BlockSpec(memory_space=pltpu.SMEM),
            pl.BlockSpec(memory_space=pltpu.SMEM),
        ],
        out_specs=pl.BlockSpec(memory_space=pltpu.VMEM),
        scratch_shapes=[
            pltpu.VMEM(grid.shape, f32),
            pltpu.VMEM(legendre.shape, jnp.bfloat16),
            pltpu.VMEM((groups, waves, rows, lat), f32),
            pltpu.VMEM((groups, waves, rows, lat), f32),
            pltpu.VMEM((waves // 2, 2, rows + 8, lat), f32),
            pltpu.VMEM((comps, 2, GROUP, width), f32),
            pltpu.VMEM((4, 2, GROUP, width), f32),
            pltpu.VMEM((groups, 2, GROUP, LANES), f32),
            pltpu.VMEM((groups, 2, GROUP, LANES), f32),
            pltpu.SemaphoreType.DMA,
            pltpu.SemaphoreType.DMA((slots,)),
            pltpu.SemaphoreType.DMA((groups, waves)),
            pltpu.SemaphoreType.DMA((groups, waves)),
            pltpu.SemaphoreType.DMA((groups, 2)),
            pltpu.SemaphoreType.DMA((groups, 2)),
        ],
        compiler_params=pltpu.CompilerParams(
            collective_id=0, has_side_effects=True, vmem_limit_bytes=48 * 1024 * 1024
        ),
    )(grid, legendre, wave_table, pole_table, pole_index)


def solution(mesh):
    in_specs = (P(None, None, "wave"), P("wave", None, None, "pole"), P(), P(), P())
    out_specs = P(None, None, "wave", "pole")
    return jax.shard_map(shards, mesh=mesh, in_specs=in_specs, out_specs=out_specs, check_vma=False)
```

time: 130 us -> 51.5 us (0.40)
  Pallas kernels: 0 us -> 46.8 us
  waiting for transfers between devices: 39.1 us -> 0 us
  blocking collectives: 21.8 us -> 0 us
  matrix products: 20.1 us -> 0 us
  other arithmetic: 17 us -> 0 us
  between operations: 13.7 us -> 0.01 us
  local copies, waits for them, and re-layouts: 12.4 us -> 3.94 us
  starting transfers between devices: 5.21 us -> 0 us
    pallas_call x0 -> x1, Pallas kernels: none -> 46.8 us  [shards(): pl.pallas_call(functools.partial(kernel, waves, poles), out_shape=jax.Sha...]
    reduce_scatter x1 -> x0, waiting for transfers between devices: 23.1 us -> none  [shards(): lax.psum_scatter(partial_terms, 'pole', scatter_dimension=3, tiled=True)]
    all_gather x1 -> x0, blocking collectives: 21.8 us -> none  [shards(): whole = lax.all_gather(spectra, 'pole', axis=3, tiled=True)]
    dot_general x3 -> x0, matrix products: 20.1 us -> none  [the longest x1 9.96 us: shards(): jnp.einsum('mpwlk,pwcml->cpmk', leg_blocks, high, preferred_element_type=...]
    all_to_all x1 -> x0, waiting for transfers between devices: 16 us -> none  [shards(): lax.all_to_all(columns[None], 'wave', split_axis=2, concat_axis=0, tiled=...]
    sub x8 -> x0, other arithmetic: 6.75 us -> none  [cmul(): return (are * bre - aim * bim, are * bim + aim * bre)]
    slice x7 -> x0, local copies, waits for them, and re-layouts: 5.74 us -> none  [solve(): ext[:, :, 1, :, 1:count + 1]]
    all_to_all x1 -> x0, starting transfers between devices: 5.17 us -> none  [shards(): lax.all_to_all(columns[None], 'wave', split_axis=2, concat_axis=0, tiled=...]
  transfers between devices with their start and end apart: 2 -> 0, of which waited for: 2 -> 0; matrix products, arithmetic and copies ran while one was open for 1% -> 0% of each run, Pallas kernels for 0% -> 0%
where the time goes in v1:
time: 51.5 us; the launch traced here: 50.8 us
  Pallas kernels  46.8 us (91%)
  local copies, waits for them, and re-layouts  3.94 us (8%)
    pallas_call x1, Pallas kernels, shards(): pl.pallas_call(functools.partial(kernel, waves, poles), out_shape=jax.Sha...  46.8 us
    unnamed x9, local copies, waits for them, and re-layouts  3.94 us

profile of v1, /device:TPU:0, one launch (start us, length us, event | category | flops | bytes accessed | tf_op | source)
XLA Modules:
  0.0 50.8 jit_solution(12206021788075461185)
XLA Ops:
  0.0 0.0 copy-start
  0.0 1.3 %copy-done = f32[6,128,384]{2,1,0:T(8,128)S(1)} copy-done((f32[6,128,384]{2,1,0:T(8,128)S(1)}, f32[6,128,384]{2,1,0:T(8,128)}, u32[]{:S(2)}) %copy-start) | copy-done | bytes 1179672
  1.3 0.0 copy-start.1
  1.3 0.7 %copy-done.1 = f32[4,32]{1,0:T(4,128)S(1)} copy-done((f32[4,32]{1,0:T(4,128)S(1)}, f32[4,32]{1,0:T(4,128)}, u32[]{:S(2)}) %copy-start.1) | copy-done | bytes 536
  2.0 0.0 copy-start.2
  2.0 0.7 %copy-done.2 = s32[128]{0:T(128)S(1)} copy-done((s32[128]{0:T(128)S(1)}, s32[128]{0:T(128)}, u32[]{:S(2)}) %copy-start.2) | copy-done | bytes 536
  2.6 0.0 copy-start.3
  2.6 0.7 %copy-done.3 = s32[16]{0:T(128)S(1)} copy-done((s32[16]{0:T(128)S(1)}, s32[16]{0:T(128)}, u32[]{:S(2)}) %copy-start.3) | copy-done | bytes 88
  3.3 46.8 %shard_map.55 = f32[6,2,16,256]{3,2,1,0:T(8,128)S(1)} custom-call(f32[6,128,384]{2,1,0:T(8,128)S(1)} %copy-done, bf16[16,2,1536,256]{3,2,1,0:T(8,128)(2,1)} %leg_hbm.1, s32[128]{0:T(128)S(1)} %copy-done.2, f32[4,32]{1,0:T(4,128)S(1)} %copy-done.1, s32[16]{0:T(128)S(1)} %copy-done.3), custom_call_target="tpu_custom_call" | custom-call | tf_op jit(solution)/shard_map/pallas_call | solution.py:334
  50.1 0.7 %copy.7 = f32[6,2,16,256]{3,2,1,0:T(8,128)} copy(f32[6,2,16,256]{3,2,1,0:T(8,128)S(1)} %shard_map.55) | data formatting | bytes 393216
Async XLA Ops:
  0.0 1.3 %copy-start = (f32[6,128,384]{2,1,0:T(8,128)S(1)}, f32[6,128,384]{2,1,0:T(8,128)}, u32[]{:S(2)}) copy-start(f32[6,128,384]{2,1,0:T(8,128)} %grid_hbm.1) | copy-start | bytes 3538948
  1.3 0.7 %copy-start.1 = (f32[4,32]{1,0:T(4,128)S(1)}, f32[4,32]{1,0:T(4,128)}, u32[]{:S(2)}) copy-start(f32[4,32]{1,0:T(4,128)} %pole_table.1) | copy-start | bytes 1540
  2.0 0.7 %copy-start.2 = (s32[128]{0:T(128)S(1)}, s32[128]{0:T(128)}, u32[]{:S(2)}) copy-start(s32[128]{0:T(128)} %wave_table.1) | copy-start | bytes 1540
  2.6 0.7 %copy-start.3 = (s32[16]{0:T(128)S(1)}, s32[16]{0:T(128)}, u32[]{:S(2)}) copy-start(s32[16]{0:T(128)} %pole_index.1) | copy-start | bytes 196

commit v2 on v1

--- a/solution.py
+++ b/solution.py
@@ -10,6 +10,7 @@
 SWEEPS = 8
 GROUP = 8
 HALO = 4
+BATCH = 4
 LANES = 128
 MESH = pl.DeviceIdType.MESH
 
@@ -72,6 +73,7 @@
     rows = GROUP * comps
     width = count + LANES
     solves = pole_index.shape[0]
+    batch = next(b for b in (BATCH, 2, 1) if solves % b == 0)
     me = lax.axis_index("wave")
     zone = lax.axis_index("pole")
 
@@ -158,15 +160,19 @@
             device_id_type=MESH,
         )
 
-    def group_step(g, carry):
+    def prepare(g, carry):
         wave = jnp.zeros((GROUP, width), jnp.float32)
         for s in range(GROUP):
             m = wave_table[me * slots + g * GROUP + s].astype(jnp.float32)
             wave = jnp.where(line == s, m, wave)
         for p in range(2):
             for i, value in enumerate(coefficients(wave, position, valid, float(p))):
-                coef[i, p] = value
-
+                coef[g, i, p] = value
+        return carry
+
+    lax.fori_loop(0, groups, prepare, 0)
+
+    def analyse_group(g, carry):
         for w in range(half):
             for source in (w, w + half):
 
@@ -184,7 +190,7 @@
             slot = g * GROUP + s
             pltpu.make_async_copy(leg_hbm.at[slot], leg_v.at[slot], leg_sem.at[slot]).wait()
 
-            def analyse(p, carry, s=s, slot=slot):
+            for p in range(2):
                 total = jnp.zeros((16, count), jnp.float32)
                 for first in range(0, half, span):
                     pieces = []
@@ -200,18 +206,15 @@
                     )
                 both = total[0:8] + total[8:16]
                 for c in range(comps):
-                    spec[c, p, s : s + 1, 0:count] = both[c : c + 1]
-                return carry
-
-            lax.fori_loop(0, 2, analyse, 0)
+                    spec[g, c, p, s : s + 1, 0:count] = both[c : c + 1]
 
         lower = jnp.zeros((GROUP, LANES), jnp.float32)
         upper = jnp.zeros((GROUP, LANES), jnp.float32)
         for i in range(2 * comps):
             c, p = i // 2, i % 2
             mine = (lane >= HALO * i) & (lane < HALO * (i + 1))
-            first = spec[c, p, :, 0:LANES]
-            last = spec[c, p, :, count - LANES : count]
+            first = spec[g, c, p, :, 0:LANES]
+            last = spec[g, c, p, :, count - LANES : count]
             lower = jnp.where(mine, pltpu.roll(first, HALO * i, 1) if i else first, lower)
             upper = jnp.where(mine, pltpu.roll(last, HALO * (i + 1), 1), upper)
         halo_send[g, 0] = lower
@@ -225,6 +228,11 @@
         def _():
             right_copy(g).start()
 
+        return carry
+
+    lax.fori_loop(0, groups, analyse_group, 0)
+
+    def solve_group(g, carry):
         @pl.when(zone > 0)
         def _():
             right_copy(g).wait_recv()
@@ -243,75 +251,88 @@
             left = pltpu.roll(from_left, LANES - HALO * (i + 1), 1)
             edge = jnp.where((lane < HALO) & (zone < poles - 1), right, 0.0)
             edge = jnp.where((lane >= LANES - HALO) & (zone > 0), left, edge)
-            spec[c, p, :, count:width] = edge
+            spec[g, c, p, :, count:width] = edge
 
         home = pl.ds(pl.multiple_of(g * GROUP, GROUP), GROUP)
         out_ref[:, :, home, :] = jnp.zeros((comps, 2, GROUP, count), jnp.float32)
 
-        def near(field):
-            even, odd = field
-            first = coef[0, 0] * pltpu.roll(odd, 1, 1) + coef[1, 0] * odd
-            second = coef[0, 1] * even + coef[1, 1] * pltpu.roll(even, width - 1, 1)
+        def near(even, odd):
+            first = coef[g, 0, 0] * pltpu.roll(odd, 1, 1) + coef[g, 1, 0] * odd
+            second = coef[g, 0, 1] * even + coef[g, 1, 1] * pltpu.roll(even, width - 1, 1)
             return first, second
 
-        def pole_step(q, carry):
-            column = pole_index[q]
-            a_re, a_im = pole_table[0, column], pole_table[1, column]
-            w_re, w_im = pole_table[2, column], pole_table[3, column]
-            inv, turn, z_first, d_first, dinv, b_all = [], [], [], [], [], []
+        def setup(a_re, a_im):
+            inv, turn, z_first, d_first = [], [], [], []
             for p in range(2):
-                rossby, grav = coef[2, p], coef[3, p]
-                b_re = a_re + 0.0 * rossby
-                b_im = a_im + rossby
+                v_re, v_im, b_re, b_im = divisor(a_re, a_im, p, width)
+                grav = coef[g, 3, p]
                 b_mag = 1.0 / (b_re * b_re + b_im * b_im)
                 i_re, i_im = b_re * b_mag, -b_im * b_mag
-                det_re, det_im = cmul(b_re, b_im, a_re, a_im)
-                det_re = det_re + grav * grav
-                det_mag = 1.0 / (det_re * det_re + det_im * det_im)
-                v_re, v_im = det_re * det_mag, -det_im * det_mag
                 t_re, t_im = cmul(a_re, a_im, v_re, v_im)
-                g_re, g_im = cmul(v_re, v_im, grav * spec[4, p], grav * spec[5, p])
-                d_re, d_im = cmul(t_re, t_im, spec[2, p], spec[3, p])
+                g_re, g_im = cmul(v_re, v_im, grav * spec[g, 4, p], grav * spec[g, 5, p])
+                d_re, d_im = cmul(t_re, t_im, spec[g, 2, p], spec[g, 3, p])
                 inv.append((i_re, i_im))
                 turn.append((t_re, t_im))
-                dinv.append((v_re, v_im))
-                b_all.append((b_re, b_im))
-                z_first.append(cmul(i_re, i_im, spec[0, p], spec[1, p]))
+                z_first.append(cmul(i_re, i_im, spec[g, 0, p], spec[g, 1, p]))
                 d_first.append((d_re + g_re, d_im + g_im))
-            z, d = z_first, d_first
+            return inv, turn, z_first, d_first
+
+        def divisor(a_re, a_im, p, upto):
+            rossby, grav = coef[g, 2, p, :, 0:upto], coef[g, 3, p, :, 0:upto]
+            b_re = a_re + 0.0 * rossby
+            b_im = a_im + rossby
+            det_re, det_im = cmul(b_re, b_im, a_re, a_im)
+            det_re = det_re + grav * grav
+            det_mag = 1.0 / (det_re * det_re + det_im * det_im)
+            return det_re * det_mag, -det_im * det_mag, b_re, b_im
+
+        def pole_step(q, carry):
+            chosen = [pole_index[q * batch + i] for i in range(batch)]
+            pole = [[pole_table[r, column] for r in range(4)] for column in chosen]
+            fixed = [setup(pole[i][0], pole[i][1]) for i in range(batch)]
+            z = [fixed[i][2] for i in range(batch)]
+            d = [fixed[i][3] for i in range(batch)]
+            zn = [None] * batch
             for sweep in range(1, SWEEPS):
-                zn_re = near((z[0][0], z[1][0]))
-                zn_im = near((z[0][1], z[1][1]))
-                dn_re = near((d[0][0], d[1][0]))
-                dn_im = near((d[0][1], d[1][1]))
-                z_next, d_next = [], []
-                for p in range(2):
-                    re, im = cmul(inv[p][0], inv[p][1], dn_re[p], dn_im[p])
-                    z_next.append((z_first[p][0] - re, z_first[p][1] - im))
-                    re, im = cmul(turn[p][0], turn[p][1], zn_re[p], zn_im[p])
-                    d_next.append((d_first[p][0] + re, d_first[p][1] + im))
-                z, d = z_next, d_next
+                for i in range(batch):
+                    inv, turn, z_first, d_first = fixed[i]
+                    zn_re = near(z[i][0][0], z[i][1][0])
+                    zn_im = near(z[i][0][1], z[i][1][1])
+                    dn_re = near(d[i][0][0], d[i][1][0])
+                    dn_im = near(d[i][0][1], d[i][1][1])
+                    z_next, d_next = [], []
+                    for p in range(2):
+                        re, im = cmul(inv[p][0], inv[p][1], dn_re[p], dn_im[p])
+                        z_next.append((z_first[p][0] - re, z_first[p][1] - im))
+                        re, im = cmul(turn[p][0], turn[p][1], zn_re[p], zn_im[p])
+                        d_next.append((d_first[p][0] + re, d_first[p][1] + im))
+                    z[i], d[i] = z_next, d_next
+                    zn[i] = (zn_re, zn_im)
             for p in range(2):
-                grav = coef[3, p][:, 0:count]
-                hb_re, hb_im = cmul(
-                    b_all[p][0][:, 0:count],
-                    b_all[p][1][:, 0:count],
-                    spec[4, p, :, 0:count],
-                    spec[5, p, :, 0:count],
-                )
-                nh_re = hb_re - grav * (spec[2, p, :, 0:count] + zn_re[p][:, 0:count])
-                nh_im = hb_im - grav * (spec[3, p, :, 0:count] + zn_im[p][:, 0:count])
-                h = cmul(nh_re, nh_im, dinv[p][0][:, 0:count], dinv[p][1][:, 0:count])
-                for f, (re, im) in enumerate((z[p], d[p], h)):
-                    o_re, o_im = cmul(w_re, w_im, re[:, 0:count], im[:, 0:count])
-                    out_ref[2 * f, p, home, :] += o_re
-                    out_ref[2 * f + 1, p, home, :] += o_im
+                grav = coef[g, 3, p, :, 0:count]
+                sums = [None] * 6
+                for i in range(batch):
+                    a_re, a_im, w_re, w_im = pole[i]
+                    v_re, v_im, b_re, b_im = divisor(a_re, a_im, p, count)
+                    hb_re, hb_im = cmul(
+                        b_re, b_im, spec[g, 4, p, :, 0:count], spec[g, 5, p, :, 0:count]
+                    )
+                    rd_re = spec[g, 2, p, :, 0:count] + zn[i][0][p][:, 0:count]
+                    rd_im = spec[g, 3, p, :, 0:count] + zn[i][1][p][:, 0:count]
+                    h = cmul(hb_re - grav * rd_re, hb_im - grav * rd_im, v_re, v_im)
+                    for f, (re, im) in enumerate((z[i][p], d[i][p], h)):
+                        term = cmul(w_re, w_im, re[:, 0:count], im[:, 0:count])
+                        for part in range(2):
+                            n = 2 * f + part
+                            sums[n] = term[part] if i == 0 else sums[n] + term[part]
+                for n in range(6):
+                    out_ref[n, p, home, :] += sums[n]
             return carry
 
-        lax.fori_loop(0, solves, pole_step, 0)
+        lax.fori_loop(0, solves // batch, pole_step, 0)
         return carry
 
-    lax.fori_loop(0, groups, group_step, 0)
+    lax.fori_loop(0, groups, solve_group, 0)
 
     for g in range(groups):
 
@@ -348,8 +369,8 @@
             pltpu.VMEM((groups, waves, rows, lat), f32),
             pltpu.VMEM((groups, waves, rows, lat), f32),
             pltpu.VMEM((waves // 2, 2, rows + 8, lat), f32),
-            pltpu.VMEM((comps, 2, GROUP, width), f32),
-            pltpu.VMEM((4, 2, GROUP, width), f32),
+            pltpu.VMEM((groups, comps, 2, GROUP, width), f32),
+            pltpu.VMEM((groups, 4, 2, GROUP, width), f32),
             pltpu.VMEM((groups, 2, GROUP, LANES), f32),
             pltpu.VMEM((groups, 2, GROUP, LANES), f32),
             pltpu.SemaphoreType.DMA,
@@ -360,7 +381,7 @@
             pltpu.SemaphoreType.DMA((groups, 2)),
         ],
         compiler_params=pltpu.CompilerParams(
-            collective_id=0, has_side_effects=True, vmem_limit_bytes=48 * 1024 * 1024
+            collective_id=0, has_side_effects=True, vmem_limit_bytes=64 * 1024 * 1024
         ),
     )(grid, legendre, wave_table, pole_table, pole_index)
 

time: 51.5 us -> 39.2 us (0.76)
  Pallas kernels: 46.8 us -> 37.3 us
  local copies, waits for them, and re-layouts: 3.94 us -> 1.62 us
    pallas_call x1, Pallas kernels: 46.8 us -> 37.3 us  [shards(): pl.pallas_call(functools.partial(kernel, waves, poles), out_shape=jax.Sha...]
    unnamed x9 -> x1, local copies, waits for them, and re-layouts: 3.94 us -> 1.62 us
where the time goes in v2:
time: 39.2 us; the launch traced here: 38.9 us
  Pallas kernels  37.3 us (95%)
  local copies, waits for them, and re-layouts  1.62 us (4%)
    pallas_call x1, Pallas kernels, shards(): pl.pallas_call(functools.partial(kernel, waves, poles), out_shape=jax.Sha...  37.3 us
    unnamed x1, local copies, waits for them, and re-layouts  1.62 us

profile of v2, /device:TPU:0, one launch (start us, length us, event | category | flops | bytes accessed | tf_op | source)
XLA Modules:
  0.0 38.9 jit_solution(231058265683569424)
XLA Ops:
  0.0 37.3 %shard_map.55 = f32[6,2,16,256]{3,2,1,0:T(8,128)} custom-call(f32[6,128,384]{2,1,0:T(8,128)} %grid_hbm.1, bf16[16,2,1536,256]{3,2,1,0:T(8,128)(2,1)} %leg_hbm.1, s32[128]{0:T(128)} %wave_table.1, f32[4,32]{1,0:T(4,128)} %pole_table.1, s32[16]{0:T(128)} %pole_index.1), custom_call_target="tpu_custom_call" | custom-call | tf_op jit(solution)/shard_map/pallas_call | solution.py:355
  37.3 1.6 %copy.7 = f32[6,2,16,256]{3,2,1,0:T(8,128)} copy(f32[6,2,16,256]{3,2,1,0:T(8,128)} %shard_map.55) | data formatting | bytes 393216

commit v3 on v2

--- a/solution.py
+++ b/solution.py
@@ -45,16 +45,12 @@
     grid_hbm,
     leg_hbm,
     wave_table,
-    pole_table,
-    pole_index,
-    out_ref,
+    spec,
     grid_v,
     leg_v,
     send,
     recv,
     parts,
-    spec,
-    coef,
     halo_send,
     halo_recv,
     grid_sem,
@@ -72,8 +68,6 @@
     half = waves // 2
     rows = GROUP * comps
     width = count + LANES
-    solves = pole_index.shape[0]
-    batch = next(b for b in (BATCH, 2, 1) if solves % b == 0)
     me = lax.axis_index("wave")
     zone = lax.axis_index("pole")
 
@@ -133,13 +127,6 @@
         collect(recv, g, me)
 
     lane = lax.broadcasted_iota(jnp.int32, (GROUP, LANES), 1)
-    line = lax.broadcasted_iota(jnp.int32, (GROUP, width), 0)
-    place = lax.broadcasted_iota(jnp.int32, (GROUP, width), 1)
-    local = jnp.where(place >= width - HALO, place - width, place)
-    k_index = local + zone * count
-    valid = (local < count + HALO) & (k_index >= 0) & (k_index < poles * count)
-    position = k_index.astype(jnp.float32)
-
     def left_copy(g):
         return pltpu.make_async_remote_copy(
             src_ref=halo_send.at[g, 0],
@@ -159,18 +146,6 @@
             device_id=(me, lax.rem(zone + 1, poles)),
             device_id_type=MESH,
         )
-
-    def prepare(g, carry):
-        wave = jnp.zeros((GROUP, width), jnp.float32)
-        for s in range(GROUP):
-            m = wave_table[me * slots + g * GROUP + s].astype(jnp.float32)
-            wave = jnp.where(line == s, m, wave)
-        for p in range(2):
-            for i, value in enumerate(coefficients(wave, position, valid, float(p))):
-                coef[g, i, p] = value
-        return carry
-
-    lax.fori_loop(0, groups, prepare, 0)
 
     def analyse_group(g, carry):
         for w in range(half):
@@ -232,7 +207,7 @@
 
     lax.fori_loop(0, groups, analyse_group, 0)
 
-    def solve_group(g, carry):
+    def place_halo(g, carry):
         @pl.when(zone > 0)
         def _():
             right_copy(g).wait_recv()
@@ -253,6 +228,47 @@
             edge = jnp.where((lane >= LANES - HALO) & (zone > 0), left, edge)
             spec[g, c, p, :, count:width] = edge
 
+        return carry
+
+    lax.fori_loop(0, groups, place_halo, 0)
+
+    for g in range(groups):
+
+        def finish(step, carry, g=g):
+            exchange(g, lax.rem(me + step, waves), me).wait_send()
+            return carry
+
+        lax.fori_loop(1, waves, finish, 0)
+
+
+def solve_kernel(poles, spec, wave_table, pole_table, pole_index, out_ref, coef):
+    groups, comps, _, _, width = spec.shape
+    count = width - LANES
+    slots = groups * GROUP
+    solves = pole_index.shape[0]
+    batch = next(b for b in (BATCH, 2, 1) if solves % b == 0)
+    me = lax.axis_index("wave")
+    zone = lax.axis_index("pole")
+    line = lax.broadcasted_iota(jnp.int32, (GROUP, width), 0)
+    place = lax.broadcasted_iota(jnp.int32, (GROUP, width), 1)
+    local = jnp.where(place >= width - HALO, place - width, place)
+    k_index = local + zone * count
+    valid = (local < count + HALO) & (k_index >= 0) & (k_index < poles * count)
+    position = k_index.astype(jnp.float32)
+
+    def prepare(g, carry):
+        wave = jnp.zeros((GROUP, width), jnp.float32)
+        for s in range(GROUP):
+            m = wave_table[me * slots + g * GROUP + s].astype(jnp.float32)
+            wave = jnp.where(line == s, m, wave)
+        for p in range(2):
+            for i, value in enumerate(coefficients(wave, position, valid, float(p))):
+                coef[g, i, p] = value
+        return carry
+
+    lax.fori_loop(0, groups, prepare, 0)
+
+    def solve_group(g, carry):
         home = pl.ds(pl.multiple_of(g * GROUP, GROUP), GROUP)
         out_ref[:, :, home, :] = jnp.zeros((comps, 2, GROUP, count), jnp.float32)
 
@@ -334,14 +350,6 @@
 
     lax.fori_loop(0, groups, solve_group, 0)
 
-    for g in range(groups):
-
-        def finish(step, carry, g=g):
-            exchange(g, lax.rem(me + step, waves), me).wait_send()
-            return carry
-
-        lax.fori_loop(1, waves, finish, 0)
-
 
 def shards(grid, legendre, wave_table, pole_table, pole_index):
     waves = lax.axis_size("wave")
@@ -352,25 +360,20 @@
     rows = GROUP * comps
     width = count + LANES
     f32 = jnp.float32
-    return pl.pallas_call(
+    anywhere = pl.BlockSpec(memory_space=pl.ANY)
+    scalars = pl.BlockSpec(memory_space=pltpu.SMEM)
+    vector = pl.BlockSpec(memory_space=pltpu.VMEM)
+    spec = pl.pallas_call(
         functools.partial(kernel, waves, poles),
-        out_shape=jax.ShapeDtypeStruct((comps, 2, slots, count), f32),
-        in_specs=[
-            pl.BlockSpec(memory_space=pl.ANY),
-            pl.BlockSpec(memory_space=pl.ANY),
-            pl.BlockSpec(memory_space=pltpu.SMEM),
-            pl.BlockSpec(memory_space=pltpu.SMEM),
-            pl.BlockSpec(memory_space=pltpu.SMEM),
-        ],
-        out_specs=pl.BlockSpec(memory_space=pltpu.VMEM),
+        out_shape=jax.ShapeDtypeStruct((groups, comps, 2, GROUP, width), f32),
+        in_specs=[anywhere, anywhere, scalars],
+        out_specs=vector,
         scratch_shapes=[
             pltpu.VMEM(grid.shape, f32),
             pltpu.VMEM(legendre.shape, jnp.bfloat16),
             pltpu.VMEM((groups, waves, rows, lat), f32),
             pltpu.VMEM((groups, waves, rows, lat), f32),
             pltpu.VMEM((waves // 2, 2, rows + 8, lat), f32),
-            pltpu.VMEM((groups, comps, 2, GROUP, width), f32),
-            pltpu.VMEM((groups, 4, 2, GROUP, width), f32),
             pltpu.VMEM((groups, 2, GROUP, LANES), f32),
             pltpu.VMEM((groups, 2, GROUP, LANES), f32),
             pltpu.SemaphoreType.DMA,
@@ -383,7 +386,15 @@
         compiler_params=pltpu.CompilerParams(
             collective_id=0, has_side_effects=True, vmem_limit_bytes=64 * 1024 * 1024
         ),
-    )(grid, legendre, wave_table, pole_table, pole_index)
+    )(grid, legendre, wave_table)
+    return pl.pallas_call(
+        functools.partial(solve_kernel, poles),
+        out_shape=jax.ShapeDtypeStruct((comps, 2, slots, count), f32),
+        in_specs=[vector, scalars, scalars, scalars],
+        out_specs=vector,
+        scratch_shapes=[pltpu.VMEM((groups, 4, 2, GROUP, width), f32)],
+        compiler_params=pltpu.CompilerParams(vmem_limit_bytes=64 * 1024 * 1024),
+    )(spec, wave_table, pole_table, pole_index)
 
 
 def solution(mesh):

time: 39.2 us -> 42.2 us (1.077)
  Pallas kernels: 37.3 us -> 42 us
  local copies, waits for them, and re-layouts: 1.62 us -> 0 us
    pallas_call x0 -> x1, Pallas kernels: none -> 10.2 us  [shards(): pl.pallas_call(functools.partial(solve_kernel, poles), out_shape=jax.Shap...]
    pallas_call x1, Pallas kernels: 37.3 us -> 31.8 us  [shards(): pl.pallas_call(functools.partial(kernel, waves, poles), out_shape=jax.Sha...]
    unnamed x1 -> x0, local copies, waits for them, and re-layouts: 1.62 us -> none
where the time goes in v3:
time: 42.2 us; the launch traced here: 42 us
  Pallas kernels  42 us (100%)
    pallas_call x1, Pallas kernels, shards(): pl.pallas_call(functools.partial(kernel, waves, poles), out_shape=jax.Sha...  31.8 us
    pallas_call x1, Pallas kernels, shards(): pl.pallas_call(functools.partial(solve_kernel, poles), out_shape=jax.Shap...  10.2 us

profile of v3, /device:TPU:0, one launch (start us, length us, event | category | flops | bytes accessed | tf_op | source)
XLA Modules:
  0.0 42.0 jit_solution(11560316164813806562)
XLA Ops:
  0.0 31.8 %shard_map.55.spec = f32[2,6,2,8,384]{4,3,2,1,0:T(8,128)} custom-call(f32[6,128,384]{2,1,0:T(8,128)} %grid_hbm.1, bf16[16,2,1536,256]{3,2,1,0:T(8,128)(2,1)} %leg_hbm.1, s32[128]{0:T(128)} %wave_table.3), custom_call_target="tpu_custom_call" | custom-call | tf_op jit(solution)/shard_map/pallas_call | solution.py:366
  31.8 10.2 %shard_map.56 = f32[6,2,16,256]{3,2,1,0:T(8,128)} custom-call(f32[2,6,2,8,384]{4,3,2,1,0:T(8,128)} %shard_map.55.spec, s32[128]{0:T(128)} %wave_table.3, f32[4,32]{1,0:T(4,128)} %pole_table.1, s32[16]{0:T(128)} %pole_index.1), custom_call_target="tpu_custom_call" | custom-call | tf_op jit(solution)/shard_map/pallas_call | solution.py:390
